TPU v7x, 512 devices: a whole 4x8x8 slice. The times are simulated.
512 devices in a mesh: dom: 128 (over z, y, core), hub: 4 (over x).
Axes of the slice: x: 4, y: 8, z: 8, core: 2. Of those that a mesh axis runs over, the one named last changes fastest.
Arguments:
- user_cot: float32 [16384, 256], P('dom'), may hold values from -6 to 6
- hub_adj: float32 [16384, 2048], P('dom', 'hub'), may hold values from -0.09375 to 0.09375
- tiles: float32 [65536, 8, 128], P(('dom', 'hub')), may hold values from -0.125 to 0.125
- tile_index: int32 [3, 65536], P(None, ('dom', 'hub')), may hold values from 0 to 127, as said below
- hub_mask: int32 [2, 2048, 256], P(None, 'hub'), may hold values 0 or 1
- tail_mask: int32 [2, 32768, 256], P(None, 'dom'), may hold values 0 or 1
Outputs:
- user_grad: float32 [16384, 256], P('dom')
- hub_grad: float32 [2048, 256], P('hub')
- tail_grad: float32 [32768, 256], P('dom')
Inputs may be any that keep to these rules, and one draw needn't show every extreme that they name: `tile_index`: row 0 is a tile's user block within its own partition (below 1), row 1 the partition that owns its items (below 128 partitions, i.e. 16384 / 128), row 2 the item block within that partition (below 32). Rows 1 and 2 are the same, position by position, on all 4 hub shards of one partition. No device holds more than 2 tiles whose items one partition owns. One particular partition receives exactly 2 tiles from every device; any other partition receives 0, 1 or 2 tiles from a device.
All inputs are finite; a program needn't handle non-finite values. No bound on the sum of `hub_mask` or of `tail_mask` on one device may be relied on, other than what follows from the above.
Results may differ from a plain program's by a relative error of at most 0.0001.
Values sent between devices are 32-bit elements; how exact they have to be, the bound alone decides.
A program may use at most 64 MiB of HBM per device.

v0:
```python
import jax
import jax.numpy as jnp
from jax import lax
from jax.sharding import PartitionSpec as P

PRECISE = lax.Precision.HIGHEST


def local(user_cot, hub_adj, tiles, tile_index, hub_mask, tail_mask):
    dom_count = lax.axis_size("dom")
    tile_count, item_rows, user_rows = tiles.shape
    user_count, feature_width = user_cot.shape
    user_blocks = user_count // user_rows
    tail_rows = tail_mask.shape[1]
    tail_blocks = tail_rows // item_rows
    capacity = max(2, 2 * tile_count // dom_count)
    slot_count = dom_count * capacity
    user_block = tile_index[0]
    owners = tile_index[1]
    item_block = tile_index[2]
    chosen = (user_block[:, None] == jnp.arange(user_blocks, dtype=jnp.int32)[None, :]).astype(
        jnp.float32
    )
    placed = (chosen[:, None, :, None] * tiles[:, :, None, :]).reshape(
        tile_count * item_rows, user_count
    )
    positions = jnp.arange(tile_count, dtype=jnp.int32)
    before = (owners[:, None] == owners[None, :]) & (positions[None, :] < positions[:, None])
    ranks = jnp.sum(before.astype(jnp.int32), axis=1)
    slot_of = owners * capacity + ranks
    slot_block = jnp.zeros((slot_count,), jnp.int32).at[slot_of].set(item_block)
    block_ids = jnp.arange(tail_blocks, dtype=jnp.int32)
    gradient = user_cot
    hub_item = None
    tail_item = None
    for trip_index in range(hub_mask.shape[0]):
        hub_part = lax.dot_general(
            hub_adj,
            gradient,
            (((0,), (0,)), ((), ())),
            precision=PRECISE,
            preferred_element_type=jnp.float32,
        )
        hub_item = lax.psum(hub_part, "dom") * hub_mask[trip_index].astype(jnp.float32)
        tile_part = jnp.dot(placed, gradient, precision=PRECISE, preferred_element_type=jnp.float32)
        tile_part = tile_part.reshape(tile_count, item_rows * feature_width)
        outgoing = (
            jnp.zeros((slot_count, item_rows * feature_width), jnp.float32)
            .at[slot_of]
            .set(tile_part)
        )
        incoming, got_block = (
            lax.all_to_all(outgoing, "dom", split_axis=0, concat_axis=0, tiled=True),
            lax.all_to_all(slot_block, "dom", split_axis=0, concat_axis=0, tiled=True),
        )
        member = (got_block[None, :] == block_ids[:, None]).astype(jnp.float32)
        tail_part = jnp.dot(member, incoming, precision=PRECISE, preferred_element_type=jnp.float32)
        tail_part = tail_part.reshape(tail_rows, feature_width)
        tail_item = lax.psum(tail_part, "hub") * tail_mask[trip_index].astype(jnp.float32)
        answer = tail_item.reshape(tail_blocks, item_rows * feature_width)[got_block]
        returned = lax.all_to_all(answer, "dom", split_axis=0, concat_axis=0, tiled=True)
        tile_item = returned[slot_of].reshape(tile_count * item_rows, feature_width)
        user_part = jnp.dot(
            hub_adj, hub_item, precision=PRECISE, preferred_element_type=jnp.float32
        )
        user_part = user_part + lax.dot_general(
            placed,
            tile_item,
            (((0,), (0,)), ((), ())),
            precision=PRECISE,
            preferred_element_type=jnp.float32,
        )
        gradient = lax.psum(user_part, "hub")
    return (gradient, hub_item, tail_item)


def solution(mesh):
    return jax.shard_map(
        local,
        mesh=mesh,
        in_specs=(
            P("dom", None),
            P("dom", "hub"),
            P(("dom", "hub"), None, None),
            P(None, ("dom", "hub")),
            P(None, "hub", None),
            P(None, "dom", None),
        ),
        out_specs=(P("dom", None), P("hub", None), P("dom", None)),
        check_vma=False,
    )
```

profile of v0, /device:TPU:8, one launch (start us, length us, event | category | flops | bytes accessed | tf_op | source)
XLA Modules:
  0.0 877.5 jit_solution(14577120800041582356)
XLA Ops:
  11.4 17.4 %all-to-all-start = ((s32[128,2,1]{1,2,0:T(1,128)}), s32[128,2,1]{1,2,0:T(1,128)S(1)}, u32[]{:S(2)}, u32[]{:S(2)}) async-start(s32[128,2,1]{1,2,0:T(1,128)} %bitcast.9), calls=%async_computation | async-start | bytes 131072 | tf_op jit(solution)/shard_map/all_to_all | solution.py:54
  33.4 2.3 all_to_all.43
  35.7 3.8 all-to-all-done
  39.5 10.0 %all-to-all-start.1 = ((f32[128,2,2048]{2,1,0:T(2,128)}), f32[128,2,2048]{2,1,0:T(2,128)S(1)}, u32[]{:S(2)}, u32[]{:S(2)}) async-start(f32[128,2,2048]{2,1,0:T(2,128)} %all_to_all.43), calls=%async_computation.1 | async-start | bytes 4194304 | tf_op jit(solution)/shard_map/all_to_all | solution.py:53
  51.1 52.4 %all-to-all-done.1 = f32[128,2,2048]{2,1,0:T(2,128)S(1)} async-done(((f32[128,2,2048]{2,1,0:T(2,128)}), f32[128,2,2048]{2,1,0:T(2,128)S(1)}, u32[]{:S(2)}, u32[]{:S(2)}) %all-to-all-start.1) | async-done | bytes 2097184 | tf_op jit(solution)/shard_map/all_to_all | solution.py:53
  103.5 2.5 all_to_all.45
  106.0 2.5 fusion.26
  109.3 45.8 %all-reduce.9.cloned.1.call-done = f32[256,256]{1,0:T(8,128)} async-done(((f32[256,256]{1,0:T(8,128)}), f32[256,256]{1,0:T(8,128)}) %all-reduce.9.cloned.1.call-update) | async-done | bytes 262160 | tf_op jit(solution)/shard_map/psum | solution.py:59
  159.9 14.9 %all-to-all-start.2 = ((f32[128,2,2048]{2,1,0:T(2,128)}), f32[128,2,2048]{2,1,0:T(2,128)}, u32[]{:S(2)}, u32[]{:S(2)}) async-start(f32[128,2,2048]{2,1,0:T(2,128)} %all_to_all.47), calls=%async_computation.2 | async-start | bytes 4194304 | tf_op jit(solution)/shard_map/all_to_all | solution.py:61
  176.4 52.4 %all-to-all-done.2 = f32[128,2,2048]{2,1,0:T(2,128)} async-done(((f32[128,2,2048]{2,1,0:T(2,128)}), f32[128,2,2048]{2,1,0:T(2,128)}, u32[]{:S(2)}, u32[]{:S(2)}) %all-to-all-start.2) | async-done | bytes 2097184 | tf_op jit(solution)/shard_map/all_to_all | solution.py:61
  228.8 2.7 all_to_all.49
  236.9 155.1 %all-reduce.7.cloned.1.call-done = f32[512,256]{1,0:T(8,128)} async-done(((f32[512,256]{1,0:T(8,128)}), f32[512,256]{1,0:T(8,128)}) %all-reduce.7.cloned.1.call-update) | async-done | bytes 524304 | tf_op jit(solution)/shard_map/psum | solution.py:44
  392.0 2.7 fusion.1
  394.7 50.2 %all-reduce.11.cloned.1.call-done = f32[128,256]{0,1:T(8,128)} async-done(((f32[128,256]{0,1:T(8,128)}), f32[128,256]{0,1:T(8,128)}) %all-reduce.11.cloned.1.call-update) | async-done | bytes 131088 | tf_op jit(solution)/shard_map/psum | solution.py:73
  448.0 2.4 scatter_custom_fusion.2
  450.4 2.3 all_to_all.50
  452.7 68.3 %all_to_all.61 = f32[128,2,2048]{2,1,0:T(2,128)} all-to-all(f32[128,2,2048]{2,1,0:T(2,128)} %all_to_all.50), channel_id=1, replica_groups=mesh['dom'=128,'hub'=4] {'dom'}, dimensions={0} | all-to-all | bytes 4194304 | tf_op jit(solution)/shard_map/all_to_all | solution.py:53
  521.0 2.7 all_to_all.52
  525.4 45.0 %all-reduce.15.cloned.1.call-done = f32[256,256]{1,0:T(8,128)} async-done(((f32[256,256]{1,0:T(8,128)}), f32[256,256]{1,0:T(8,128)}) %all-reduce.15.cloned.1.call-update) | async-done | bytes 262160 | tf_op jit(solution)/shard_map/psum | solution.py:59
  573.0 2.3 all_to_all.53
  575.3 14.7 %all-to-all-start.4 = ((f32[128,2,2048]{2,1,0:T(2,128)}), f32[128,2,2048]{2,1,0:T(2,128)}, u32[]{:S(2)}, u32[]{:S(2)}) async-start(f32[128,2,2048]{2,1,0:T(2,128)} %all_to_all.53), calls=%async_computation.4 | async-start | bytes 4194304 | tf_op jit(solution)/shard_map/all_to_all | solution.py:61
  591.7 215.6 %all-reduce.13.cloned.1.call-done = f32[512,256]{0,1:T(8,128)} async-done(((f32[512,256]{0,1:T(8,128)}), f32[512,256]{0,1:T(8,128)}) %all-reduce.13.cloned.1.call-update) | async-done | bytes 524304 | tf_op jit(solution)/shard_map/psum | solution.py:44
  809.3 2.7 all_to_all.55
  819.5 49.2 %all-reduce.17.cloned.1.call-done = f32[128,256]{0,1:T(8,128)} async-done(((f32[128,256]{0,1:T(8,128)}), f32[128,256]{0,1:T(8,128)}) %all-reduce.17.cloned.1.call-update) | async-done | bytes 131088 | tf_op jit(solution)/shard_map/psum | solution.py:73
  (72 shorter events, 42.2 us)
Async XLA Ops:
  8.0 166.9 %copy-start = (f32[128,512]{1,0:T(8,128)S(1)}, f32[128,512]{1,0:T(8,128)}, u32[]{:S(2)}) copy-start(f32[128,512]{1,0:T(8,128)} %param.7) | copy-start | bytes 786436
  11.4 28.1 %all-to-all-start = ((s32[128,2,1]{1,2,0:T(1,128)}), s32[128,2,1]{1,2,0:T(1,128)S(1)}, u32[]{:S(2)}, u32[]{:S(2)}) async-start(s32[128,2,1]{1,2,0:T(1,128)} %bitcast.9), calls=%async_computation | async-start | bytes 131072 | tf_op jit(solution)/shard_map/all_to_all | solution.py:54
  39.5 64.0 %all-to-all-start.1 = ((f32[128,2,2048]{2,1,0:T(2,128)}), f32[128,2,2048]{2,1,0:T(2,128)S(1)}, u32[]{:S(2)}, u32[]{:S(2)}) async-start(f32[128,2,2048]{2,1,0:T(2,128)} %all_to_all.43), calls=%async_computation.1 | async-start | bytes 4194304 | tf_op jit(solution)/shard_map/all_to_all | solution.py:53
  49.5 105.6 %all-reduce.9.cloned.1.call-start = ((), (), s32[]{:S(2)}) async-start(), calls=%async_computation.6 | async-start | bytes 524288 | tf_op jit(solution)/shard_map/psum | solution.py:59
  106.0 49.1 %copy-start.5 = (s32[2,256,256]{2,1,0:T(8,128)S(1)}, s32[2,256,256]{2,1,0:T(8,128)}, u32[]{:S(2)}) copy-start(s32[2,256,256]{2,1,0:T(8,128)} %param.11) | copy-start | bytes 1572868
  159.9 15.0 %copy-start.6 = (f32[128,256]{1,0:T(8,128)S(1)}, f32[128,256]{1,0:T(8,128)}, u32[]{:S(2)}) copy-start(f32[128,256]{1,0:T(8,128)} %param.6) | copy-start | bytes 393220
  159.9 68.9 %all-to-all-start.2 = ((f32[128,2,2048]{2,1,0:T(2,128)}), f32[128,2,2048]{2,1,0:T(2,128)}, u32[]{:S(2)}, u32[]{:S(2)}) async-start(f32[128,2,2048]{2,1,0:T(2,128)} %all_to_all.47), calls=%async_computation.2 | async-start | bytes 4194304 | tf_op jit(solution)/shard_map/all_to_all | solution.py:61
  174.8 217.2 %all-reduce.7.cloned.1.call-start = ((), (), s32[]{:S(2)}) async-start(), calls=%async_computation.5 | async-start | bytes 1048576 | tf_op jit(solution)/shard_map/psum | solution.py:44
  176.3 268.6 %all-reduce.11.cloned.1.call-start = ((), (), s32[]{:S(2)}) async-start(), calls=%async_computation.7 | async-start | bytes 262144 | tf_op jit(solution)/shard_map/psum | solution.py:73
  233.4 1.5 copy-start.1
  233.4 158.6 %copy-start.3 = (s32[2,512,256]{2,1,0:T(8,128)S(1)}, s32[2,512,256]{2,1,0:T(8,128)}, u32[]{:S(2)}) copy-start(s32[2,512,256]{2,1,0:T(8,128)} %param.10) | copy-start | bytes 3145732
  394.7 175.7 %all-reduce.15.cloned.1.call-start = ((), (), s32[]{:S(2)}) async-start(), calls=%async_computation.9 | async-start | bytes 524288 | tf_op jit(solution)/shard_map/psum | solution.py:59
  571.5 1.5 copy-start.4
  575.3 14.8 %copy-start.7 = (f32[128,256]{0,1:T(8,128)S(1)}, f32[128,256]{0,1:T(8,128)}, u32[]{:S(2)}) copy-start(f32[128,256]{0,1:T(8,128)} %all-reduce.11.cloned.1.call-done) | copy-start | bytes 393220
  575.3 234.0 %all-to-all-start.4 = ((f32[128,2,2048]{2,1,0:T(2,128)}), f32[128,2,2048]{2,1,0:T(2,128)}, u32[]{:S(2)}, u32[]{:S(2)}) async-start(f32[128,2,2048]{2,1,0:T(2,128)} %all_to_all.53), calls=%async_computation.4 | async-start | bytes 4194304 | tf_op jit(solution)/shard_map/all_to_all | solution.py:61
  590.0 1.5 slice-start
  590.0 217.3 %all-reduce.13.cloned.1.call-start = ((), (), s32[]{:S(2)}) async-start(), calls=%async_computation.8 | async-start | bytes 1048576 | tf_op jit(solution)/shard_map/psum | solution.py:44
  591.5 277.3 %all-reduce.17.cloned.1.call-start = ((), (), s32[]{:S(2)}) async-start(), calls=%async_computation.10 | async-start | bytes 262144 | tf_op jit(solution)/shard_map/psum | solution.py:73
  813.9 3.4 copy-start.2
Sparse Core Ops, SparseCore 0:
  109.4 45.6 all-reduce.8
  394.8 50.0 all-reduce.10
  525.5 44.8 all-reduce.14
  818.7 50.0 all-reduce.16
Sparse Core Ops, SparseCore 1:
  179.4 212.5 all-reduce.6
  594.6 212.6 all-reduce.12
where the time goes:
time: 879 us; the launch traced here: 878 us
  waiting for transfers between devices  669 us (76%)
  blocking collectives  68.3 us (8%)
  starting transfers between devices  57.3 us (7%)
  local copies, waits for them, and re-layouts  42.6 us (5%)
  matrix products  18 us (2%)
  between operations  15.5 us (2%)
    psum x2, waiting for transfers between devices, local(): lax.psum(hub_part, 'dom') * hub_mask[trip_index].astype(jnp.float32)  371 us
    psum x2, waiting for transfers between devices, local(): gradient = lax.psum(user_part, 'hub')  99.4 us
    psum x2, waiting for transfers between devices, local(): lax.psum(tail_part, 'hub') * tail_mask[trip_index].astype(jnp.float32)  90.8 us
    all_to_all x1, blocking collectives, local(): lax.all_to_all(outgoing, 'dom', split_axis=0, concat_axis=0, tiled=True)  68.3 us
    all_to_all x1, waiting for transfers between devices, local(): lax.all_to_all(outgoing, 'dom', split_axis=0, concat_axis=0, tiled=True)  52.4 us
    all_to_all x2, waiting for transfers between devices, local(): lax.all_to_all(answer, 'dom', split_axis=0, concat_axis=0, tiled=True)  52.4 us
    all_to_all x2, starting transfers between devices, local(): lax.all_to_all(answer, 'dom', split_axis=0, concat_axis=0, tiled=True)  29.7 us
  transfers between devices with their start and end apart: 10, of which 9 were waited for; matrix products, arithmetic and copies ran while one was open for 2% of the time, Pallas kernels for 0%

commit v1 on v0

--- a/solution.py
+++ b/solution.py
@@ -70,7 +70,7 @@
             precision=PRECISE,
             preferred_element_type=jnp.float32,
         )
-        gradient = lax.psum(user_part, "hub")
+        gradient = jnp.sum(lax.all_gather(user_part, "hub"), axis=0)
     return (gradient, hub_item, tail_item)
 
 

time: 879 us -> 802 us (0.912)
  the two profiles are of different devices: /device:TPU:8 before, /device:TPU:26 now
where the time goes in v1:
time: 802 us; the launch traced here: 801 us
  waiting for transfers between devices  575 us (72%)
  blocking collectives  88.3 us (11%)
  starting transfers between devices  58.3 us (7%)
  local copies, waits for them, and re-layouts  42 us (5%)
  matrix products  15.8 us (2%)
  between operations  15.8 us (2%)
    psum x2, waiting for transfers between devices, local(): lax.psum(hub_part, 'dom') * hub_mask[trip_index].astype(jnp.float32)  378 us
    psum x2, waiting for transfers between devices, local(): lax.psum(tail_part, 'hub') * tail_mask[trip_index].astype(jnp.float32)  92.5 us
    all_to_all x1, blocking collectives, local(): lax.all_to_all(outgoing, 'dom', split_axis=0, concat_axis=0, tiled=True)  61.4 us
    all_to_all x2, waiting for transfers between devices, local(): lax.all_to_all(answer, 'dom', split_axis=0, concat_axis=0, tiled=True)  50.8 us
    all_to_all x1, waiting for transfers between devices, local(): lax.all_to_all(outgoing, 'dom', split_axis=0, concat_axis=0, tiled=True)  50.8 us
    all_to_all x2, starting transfers between devices, local(): lax.all_to_all(answer, 'dom', split_axis=0, concat_axis=0, tiled=True)  29.4 us
    all_gather x2, blocking collectives, local(): gradient = jnp.sum(lax.all_gather(user_part, 'hub'), axis=0)  26.9 us
    all_to_all x1, starting transfers between devices, local(): lax.all_to_all(slot_block, 'dom', split_axis=0, concat_axis=0, tiled=True)  17.1 us
  transfers between devices with their start and end apart: 8, of which 7 were waited for; matrix products, arithmetic and copies ran while one was open for 2% of the time, Pallas kernels for 0%

profile of v1, /device:TPU:26, one launch (start us, length us, event | category | flops | bytes accessed | tf_op | source)
XLA Modules:
  0.0 801.2 jit_solution(16757923567548699545)
XLA Ops:
  11.4 17.1 %all-to-all-start = ((s32[128,2,1]{1,2,0:T(1,128)}), s32[128,2,1]{1,2,0:T(1,128)S(1)}, u32[]{:S(2)}, u32[]{:S(2)}) async-start(s32[128,2,1]{1,2,0:T(1,128)} %bitcast.9), calls=%async_computation | async-start | bytes 131072 | tf_op jit(solution)/shard_map/all_to_all | solution.py:54
  33.2 2.3 all_to_all.43
  35.5 2.2 all-to-all-done
  37.8 11.5 %all-to-all-start.1 = ((f32[128,2,2048]{2,1,0:T(2,128)}), f32[128,2,2048]{2,1,0:T(2,128)S(1)}, u32[]{:S(2)}, u32[]{:S(2)}) async-start(f32[128,2,2048]{2,1,0:T(2,128)} %all_to_all.43), calls=%async_computation.1 | async-start | bytes 4194304 | tf_op jit(solution)/shard_map/all_to_all | solution.py:53
  50.9 50.8 %all-to-all-done.1 = f32[128,2,2048]{2,1,0:T(2,128)S(1)} async-done(((f32[128,2,2048]{2,1,0:T(2,128)}), f32[128,2,2048]{2,1,0:T(2,128)S(1)}, u32[]{:S(2)}, u32[]{:S(2)}) %all-to-all-start.1) | async-done | bytes 2097184 | tf_op jit(solution)/shard_map/all_to_all | solution.py:53
  101.7 2.5 all_to_all.45
  104.2 2.5 fusion.26
  107.5 46.3 %all-reduce.7.cloned.1.call-done = f32[256,256]{1,0:T(8,128)} async-done(((f32[256,256]{1,0:T(8,128)}), f32[256,256]{1,0:T(8,128)}) %all-reduce.7.cloned.1.call-update) | async-done | bytes 262160 | tf_op jit(solution)/shard_map/psum | solution.py:59
  156.3 2.2 all_to_all.47
  158.6 14.9 %all-to-all-start.2 = ((f32[128,2,2048]{2,1,0:T(2,128)}), f32[128,2,2048]{2,1,0:T(2,128)}, u32[]{:S(2)}, u32[]{:S(2)}) async-start(f32[128,2,2048]{2,1,0:T(2,128)} %all_to_all.47), calls=%async_computation.2 | async-start | bytes 4194304 | tf_op jit(solution)/shard_map/all_to_all | solution.py:61
  175.0 50.8 %all-to-all-done.2 = f32[128,2,2048]{2,1,0:T(2,128)} async-done(((f32[128,2,2048]{2,1,0:T(2,128)}), f32[128,2,2048]{2,1,0:T(2,128)}, u32[]{:S(2)}, u32[]{:S(2)}) %all-to-all-start.2) | async-done | bytes 2097184 | tf_op jit(solution)/shard_map/all_to_all | solution.py:61
  225.9 2.7 all_to_all.49
  234.0 159.9 %all-reduce.5.cloned.1.call-done = f32[512,256]{1,0:T(8,128)} async-done(((f32[512,256]{1,0:T(8,128)}), f32[512,256]{1,0:T(8,128)}) %all-reduce.5.cloned.1.call-update) | async-done | bytes 524304 | tf_op jit(solution)/shard_map/psum | solution.py:44
  395.9 13.5 %all-gather = f32[512,256]{0,1:T(8,128)S(1)} all-gather(f32[128,256]{0,1:T(8,128)S(1)} %fusion.1), channel_id=2, replica_groups=mesh['dom'=128,'hub'=4] {'hub'}, dimensions={0}, use_global_device_ids=true | all-gather | bytes 655360 | tf_op jit(solution)/shard_map/all_gather | solution.py:73
  412.0 2.4 scatter_custom_fusion.2
  414.5 2.3 all_to_all.50
  416.8 61.4 %all_to_all.61 = f32[128,2,2048]{2,1,0:T(2,128)} all-to-all(f32[128,2,2048]{2,1,0:T(2,128)} %all_to_all.50), channel_id=1, replica_groups=mesh['dom'=128,'hub'=4] {'dom'}, dimensions={0} | all-to-all | bytes 4194304 | tf_op jit(solution)/shard_map/all_to_all | solution.py:53
  478.2 2.7 all_to_all.52
  482.5 46.1 %all-reduce.11.cloned.1.call-done = f32[256,256]{1,0:T(8,128)} async-done(((f32[256,256]{1,0:T(8,128)}), f32[256,256]{1,0:T(8,128)}) %all-reduce.11.cloned.1.call-update) | async-done | bytes 262160 | tf_op jit(solution)/shard_map/psum | solution.py:59
  531.2 2.2 all_to_all.53
  533.5 14.6 %all-to-all-start.4 = ((f32[128,2,2048]{2,1,0:T(2,128)}), f32[128,2,2048]{2,1,0:T(2,128)}, u32[]{:S(2)}, u32[]{:S(2)}) async-start(f32[128,2,2048]{2,1,0:T(2,128)} %all_to_all.53), calls=%async_computation.4 | async-start | bytes 4194304 | tf_op jit(solution)/shard_map/all_to_all | solution.py:61
  549.7 218.6 %all-reduce.9.cloned.1.call-done = f32[512,256]{0,1:T(8,128)} async-done(((f32[512,256]{0,1:T(8,128)}), f32[512,256]{0,1:T(8,128)}) %all-reduce.9.cloned.1.call-update) | async-done | bytes 524304 | tf_op jit(solution)/shard_map/psum | solution.py:44
  770.4 2.7 all_to_all.55
  779.1 13.5 %all-gather.1 = f32[512,256]{0,1:T(8,128)S(1)} all-gather(f32[128,256]{0,1:T(8,128)S(1)} %fusion), channel_id=3, replica_groups=mesh['dom'=128,'hub'=4] {'hub'}, dimensions={0}, use_global_device_ids=true | all-gather | bytes 655360 | tf_op jit(solution)/shard_map/all_gather | solution.py:73
  (72 shorter events, 39.7 us)
Async XLA Ops:
  8.0 165.5 %copy-start = (f32[128,512]{1,0:T(8,128)S(1)}, f32[128,512]{1,0:T(8,128)}, u32[]{:S(2)}) copy-start(f32[128,512]{1,0:T(8,128)} %param.7) | copy-start | bytes 786436
  11.4 26.4 %all-to-all-start = ((s32[128,2,1]{1,2,0:T(1,128)}), s32[128,2,1]{1,2,0:T(1,128)S(1)}, u32[]{:S(2)}, u32[]{:S(2)}) async-start(s32[128,2,1]{1,2,0:T(1,128)} %bitcast.9), calls=%async_computation | async-start | bytes 131072 | tf_op jit(solution)/shard_map/all_to_all | solution.py:54
  37.8 63.9 %all-to-all-start.1 = ((f32[128,2,2048]{2,1,0:T(2,128)}), f32[128,2,2048]{2,1,0:T(2,128)S(1)}, u32[]{:S(2)}, u32[]{:S(2)}) async-start(f32[128,2,2048]{2,1,0:T(2,128)} %all_to_all.43), calls=%async_computation.1 | async-start | bytes 4194304 | tf_op jit(solution)/shard_map/all_to_all | solution.py:53
  49.3 104.6 %all-reduce.7.cloned.1.call-start = ((), (), s32[]{:S(2)}) async-start(), calls=%async_computation.6 | async-start | bytes 524288 | tf_op jit(solution)/shard_map/psum | solution.py:59
  104.2 49.7 %copy-start.6 = (s32[2,256,256]{2,1,0:T(8,128)S(1)}, s32[2,256,256]{2,1,0:T(8,128)}, u32[]{:S(2)}) copy-start(s32[2,256,256]{2,1,0:T(8,128)} %param.11) | copy-start | bytes 1572868
  158.6 15.0 %copy-start.7 = (f32[128,256]{1,0:T(8,128)S(1)}, f32[128,256]{1,0:T(8,128)}, u32[]{:S(2)}) copy-start(f32[128,256]{1,0:T(8,128)} %param.6) | copy-start | bytes 393220
  158.6 67.3 %all-to-all-start.2 = ((f32[128,2,2048]{2,1,0:T(2,128)}), f32[128,2,2048]{2,1,0:T(2,128)}, u32[]{:S(2)}, u32[]{:S(2)}) async-start(f32[128,2,2048]{2,1,0:T(2,128)} %all_to_all.47), calls=%async_computation.2 | async-start | bytes 4194304 | tf_op jit(solution)/shard_map/all_to_all | solution.py:61
  173.5 220.4 %all-reduce.5.cloned.1.call-start = ((), (), s32[]{:S(2)}) async-start(), calls=%async_computation.5 | async-start | bytes 1048576 | tf_op jit(solution)/shard_map/psum | solution.py:44
  175.0 353.7 %all-reduce.11.cloned.1.call-start = ((), (), s32[]{:S(2)}) async-start(), calls=%async_computation.8 | async-start | bytes 524288 | tf_op jit(solution)/shard_map/psum | solution.py:59
  230.5 1.5 copy-start.1
  230.5 163.3 %copy-start.4 = (s32[2,512,256]{2,1,0:T(8,128)S(1)}, s32[2,512,256]{2,1,0:T(8,128)}, u32[]{:S(2)}) copy-start(s32[2,512,256]{2,1,0:T(8,128)} %param.10) | copy-start | bytes 3145732
  529.7 1.5 copy-start.5
  533.5 237.0 %all-to-all-start.4 = ((f32[128,2,2048]{2,1,0:T(2,128)}), f32[128,2,2048]{2,1,0:T(2,128)}, u32[]{:S(2)}, u32[]{:S(2)}) async-start(f32[128,2,2048]{2,1,0:T(2,128)} %all_to_all.53), calls=%async_computation.4 | async-start | bytes 4194304 | tf_op jit(solution)/shard_map/all_to_all | solution.py:61
  548.1 1.5 slice-start
  548.1 220.2 %all-reduce.9.cloned.1.call-start = ((), (), s32[]{:S(2)}) async-start(), calls=%async_computation.7 | async-start | bytes 1048576 | tf_op jit(solution)/shard_map/psum | solution.py:44
  769.4 1.0 copy-start.2
  775.1 3.4 copy-start.3
Sparse Core Ops, SparseCore 0:
  107.6 46.2 all-reduce.6
  482.6 45.9 all-reduce.10
Sparse Core Ops, SparseCore 1:
  178.1 215.7 all-reduce.4
  552.4 215.9 all-reduce.8
